TPU v7x, 512 devices: a whole 4x4x16 slice. The times are simulated.
512 devices in a mesh: dp: 4 (over x), expert: 16 (over z), tensor: 8 (over y, core).
Axes of the slice: x: 4, y: 4, z: 16, core: 2. Of those that a mesh axis runs over, the one named last changes fastest.
Arguments:
- tokens: bfloat16 [1024, 4096], P(('dp', 'expert'), 'tensor'), may hold values from -6 to 6
- expert_ids: int32 [1024, 3], P(('dp', 'expert')), may hold values from 0 to 15, all different within a row; in each aligned block of 16 rows (0 to 15, 16 to 31, ...) at most 4 rows name the same one
- route_weights: float32 [1024, 3], P(('dp', 'expert')), may hold values from 0.1 to 1
- gate_weight: bfloat16 [16, 5120, 4096], P('expert', ('dp', 'tensor')), may hold values from -0.09375 to 0.09375
- up_weight: bfloat16 [16, 5120, 4096], P('expert', ('dp', 'tensor')), may hold values from -0.09375 to 0.09375
- down_weight: bfloat16 [16, 5120, 4096], P('expert', ('dp', 'tensor')), may hold values from -0.15625 to 0.15625
Outputs:
- mixed: bfloat16 [1024, 4096], P(('dp', 'expert'), 'tensor')
Inputs may be any that keep to these rules, and one draw needn't show every extreme that they name: `expert_ids`: A row's 3 ids differ. In the rows of one device (aligned blocks of 16 rows) no expert is picked by more than 4 rows, and in every block some expert is picked by exactly 4 rows.
All inputs are finite; a program needn't handle non-finite values.
Results may differ from a plain program's by a relative error of at most 0.02.
Values may be sent and summed in bfloat16 or wider, within the bound.
A program may use at most 64 MiB of HBM per device.

v0:
```python
import jax
import jax.numpy as jnp
from jax import lax
from jax.sharding import PartitionSpec as P


def on_device(tokens, expert_ids, route_weights, gate_weight, up_weight, down_weight):
    groups = lax.axis_size("expert")
    dp_count = lax.axis_size("dp")
    rows = tokens.shape[0]
    picks = expert_ids.shape[1]
    capacity = min(rows, 4 * rows * picks // (3 * groups))
    slots = groups * capacity
    flat_ids = expert_ids.reshape(-1)
    count = flat_ids.shape[0]
    onehot = (flat_ids[:, None] == jnp.arange(groups, dtype=jnp.int32)[None, :]).astype(jnp.float32)
    earlier = (jnp.arange(count)[:, None] > jnp.arange(count)[None, :]).astype(jnp.float32)
    before = jnp.dot(earlier, onehot, precision=lax.Precision.HIGHEST)
    place = jnp.sum(before * onehot, axis=1).astype(jnp.int32)
    target = (flat_ids * capacity + place).reshape(rows, picks)
    positions = jnp.arange(slots, dtype=jnp.int32)
    matches = target[:, :, None] == positions[None, None, :]
    select = jnp.transpose(jnp.any(matches, axis=1)).astype(jnp.bfloat16)
    combine = jnp.sum(jnp.where(matches, route_weights[:, :, None], 0.0), axis=1)
    inner = down_weight.shape[1]
    full_rows = lax.all_gather(tokens, "tensor", axis=1, tiled=True)
    outgoing = jnp.dot(select, full_rows, preferred_element_type=jnp.float32).astype(jnp.bfloat16)
    arrived = lax.all_to_all(outgoing, "expert", split_axis=0, concat_axis=0, tiled=True)
    row_block = lax.all_gather(arrived, "dp", axis=0, tiled=True)
    dims = (((1,), (1,)), ((), ()))
    gate = lax.dot_general(row_block, gate_weight[0], dims, preferred_element_type=jnp.float32)
    up_part = lax.dot_general(row_block, up_weight[0], dims, preferred_element_type=jnp.float32)
    hidden = (jax.nn.silu(gate) * up_part).astype(jnp.bfloat16)
    terms = jnp.einsum(
        "nsf,fd->snd",
        hidden.reshape(dp_count, slots, inner),
        down_weight[0],
        preferred_element_type=jnp.float32,
    )
    summed = lax.psum_scatter(
        terms.reshape(slots, -1).astype(jnp.bfloat16),
        ("dp", "tensor"),
        scatter_dimension=1,
        tiled=True,
    )
    returned = lax.all_to_all(summed, "expert", split_axis=0, concat_axis=0, tiled=True)
    mixed = jnp.dot(combine, returned.astype(jnp.float32), precision=lax.Precision.HIGHEST)
    return mixed.astype(jnp.bfloat16)


def solution(mesh):
    placed = (
        P(("dp", "expert"), "tensor"),
        P(("dp", "expert"), None),
        P(("dp", "expert"), None),
        P("expert", ("dp", "tensor"), None),
        P("expert", ("dp", "tensor"), None),
        P("expert", ("dp", "tensor"), None),
    )
    return jax.shard_map(
        on_device,
        mesh=mesh,
        in_specs=placed,
        out_specs=P(("dp", "expert"), "tensor"),
        check_vma=False,
    )
```

profile of v0, /device:TPU:1, one launch (start us, length us, event | category | flops | bytes accessed | tf_op | source)
XLA Modules:
  0.0 241.5 jit_solution(1097595116934424215)
XLA Ops:
  6.5 0.0 copy-start
  6.5 0.0 all-gather.2.cloned.1.call-start
  6.5 0.9 copy.21
  7.4 0.1 eq.28
  7.5 0.1 fusion.12
  7.6 0.1 convert_element_type.31
  7.7 0.1 copy.22
  7.8 0.7 multiply_add_fusion
  8.5 0.1 fusion.13
  8.6 19.7 %all_gather.6 = bf16[16,4096]{1,0:T(8,128)(2,1)S(1)} all-gather(bf16[16,512]{1,0:T(8,128)(2,1)} %param.6), channel_id=1, replica_groups=mesh['dp'=4,'expert'=16,'tensor'=8] {'tensor'}, dimensions={1}, use_global_device_ids=true | all-gather | bytes 147456 | tf_op jit(solution)/shard_map/all_gather | solution.py:26
  28.3 0.3 convolution_convert_fusion.1
  28.6 0.2 all_to_all.16
  28.8 32.9 %all_to_all.24 = bf16[16,4,4096]{2,1,0:T(4,128)(2,1)S(1)} all-to-all(bf16[16,4,4096]{2,1,0:T(4,128)(2,1)S(1)} %all_to_all.16), channel_id=1, replica_groups=mesh['dp'=4,'expert'=16,'tensor'=8] {'expert'}, dimensions={0} | all-to-all | bytes 1048576 | tf_op jit(solution)/shard_map/all_to_all | solution.py:28
  61.7 0.0 copy-start.2
  61.7 0.9 all_to_all.18
  62.6 0.0 all-gather.2.cloned.1.call-update
  62.6 0.0 reduce-scatter.2.cloned.1.call-start
  62.7 39.8 %all-gather.2.cloned.1.call-done = bf16[256,4096]{1,0:T(8,128)(2,1)} async-done(((bf16[64,4096]{1,0:T(8,128)(2,1)}), bf16[256,4096]{1,0:T(8,128)(2,1)}) %all-gather.2.cloned.1.call-update) | async-done | bytes 2097168 | tf_op jit(solution)/shard_map/all_gather | solution.py:29
  102.5 0.0 copy-done.2
  102.5 0.0 copy-start.1
  102.5 0.0 copy-start.4
  102.5 2.6 %fusion.4 = f32[256,160]{0,1:T(8,128)S(1)} fusion(bf16[256,4096]{1,0:T(8,128)(2,1)} %all-gather.2.cloned.1.call-done, bf16[1,160,4096]{2,1,0:T(8,128)(2,1)S(1)} %copy-done.2), kind=kOutput, calls=%fused_computation.6 | convolution fusion | flops 335544320 | bytes 3571712 | tf_op jit(solution)/shard_map/dot_general | solution.py:31
  105.1 0.0 copy-done.1
  105.1 0.0 copy-done.4
  105.1 0.9 fusion.9
  106.0 0.1 copy.23
  106.1 0.0 copy-done
  106.1 0.7 fusion
  106.8 1.5 copy.25
  108.3 0.0 copy-start.3
  108.3 0.0 reduce-scatter.2.cloned.1.call-update
  108.3 100.6 %reduce-scatter.2.cloned.1.call-done = bf16[64,512]{1,0:T(8,128)(2,1)} async-done(((bf16[64,16384]{1,0:T(8,128)(2,1)}), bf16[64,512]{1,0:T(8,128)(2,1)}) %reduce-scatter.2.cloned.1.call-update) | async-done | bytes 65552 | tf_op jit(solution)/shard_map/reduce_scatter | solution.py:40
  208.9 1.5 all_to_all.19
  210.4 12.0 %all-to-all-start.1 = ((bf16[16,4,512]{2,1,0:T(4,128)(2,1)}), bf16[16,4,512]{2,1,0:T(4,128)(2,1)S(1)}, u32[]{:S(2)}, u32[]{:S(2)}) async-start(bf16[16,4,512]{2,1,0:T(4,128)(2,1)} %all_to_all.19), calls=%async_computation.2 | async-start | bytes 131072 | tf_op jit(solution)/shard_map/all_to_all | solution.py:46
  222.4 0.0 copy-done.3
  222.4 0.1 select_reduce_fusion
  222.4 11.5 %all-to-all-done.1 = bf16[16,4,512]{2,1,0:T(4,128)(2,1)S(1)} async-done(((bf16[16,4,512]{2,1,0:T(4,128)(2,1)}), bf16[16,4,512]{2,1,0:T(4,128)(2,1)S(1)}, u32[]{:S(2)}, u32[]{:S(2)}) %all-to-all-start.1) | async-done | bytes 65568 | tf_op jit(solution)/shard_map/all_to_all | solution.py:46
  233.9 0.8 convolution_convert_fusion.2
  (2 shorter events, 0.0 us)
Async XLA Ops:
  6.5 99.6 %copy-start = (bf16[1,160,4096]{2,1,0:T(8,128)(2,1)S(1)}, bf16[1,160,4096]{2,1,0:T(8,128)(2,1)}, u32[]{:S(2)}) copy-start(bf16[1,160,4096]{2,1,0:T(8,128)(2,1)} %param.11) | copy-start | bytes 3932164
  6.5 96.0 %all-gather.2.cloned.1.call-start = ((), (), s32[]{:S(2)}) async-start(), calls=%async_computation.3 | async-start | bytes 2621440 | tf_op jit(solution)/shard_map/all_gather | solution.py:29
  61.7 40.8 %copy-start.2 = (bf16[1,160,4096]{2,1,0:T(8,128)(2,1)S(1)}, bf16[1,160,4096]{2,1,0:T(8,128)(2,1)}, u32[]{:S(2)}) copy-start(bf16[1,160,4096]{2,1,0:T(8,128)(2,1)} %param.9) | copy-start | bytes 3932164
  62.6 146.3 %reduce-scatter.2.cloned.1.call-start = ((), (), s32[]{:S(2)}) async-start(), calls=%async_computation.4 | async-start | bytes 2162688 | tf_op jit(solution)/shard_map/reduce_scatter | solution.py:40
  102.5 2.6 %copy-start.1 = (bf16[256,4096]{1,0:T(8,128)(2,1)S(1)}, bf16[256,4096]{1,0:T(8,128)(2,1)}, u32[]{:S(2)}) copy-start(bf16[256,4096]{1,0:T(8,128)(2,1)} %all-gather.2.cloned.1.call-done) | copy-start | bytes 6291460
  102.5 2.6 %copy-start.4 = (bf16[1,160,4096]{2,1,0:T(8,128)(2,1)S(1)}, bf16[1,160,4096]{2,1,0:T(8,128)(2,1)}, u32[]{:S(2)}) copy-start(bf16[1,160,4096]{2,1,0:T(8,128)(2,1)} %param.10) | copy-start | bytes 3932164
  108.3 114.1 %copy-start.3 = (f32[16,3]{0,1:T(4,128)S(1)}, f32[16,3]{0,1:T(4,128)}, u32[]{:S(2)}) copy-start(f32[16,3]{0,1:T(4,128)} %param.8) | copy-start | bytes 580
  210.4 23.6 %all-to-all-start.1 = ((bf16[16,4,512]{2,1,0:T(4,128)(2,1)}), bf16[16,4,512]{2,1,0:T(4,128)(2,1)S(1)}, u32[]{:S(2)}, u32[]{:S(2)}) async-start(bf16[16,4,512]{2,1,0:T(4,128)(2,1)} %all_to_all.19), calls=%async_computation.2 | async-start | bytes 131072 | tf_op jit(solution)/shard_map/all_to_all | solution.py:46
Sparse Core Ops, SparseCore 0:
  62.7 39.7 all-gather.1
  108.4 100.4 reduce-scatter.1
where the time goes:
time: 244 us; the launch traced here: 242 us
  waiting for transfers between devices  152 us (62%)
  blocking collectives  52.5 us (22%)
  between operations  13.5 us (6%)
  starting transfers between devices  12 us (5%)
  matrix products  5.38 us (2%)
  local copies, waits for them, and re-layouts  5.32 us (2%)
    reduce_scatter x1, waiting for transfers between devices, on_device(): lax.psum_scatter(terms.reshape(slots, -1).astype(jnp.bfloat16), ('dp', 't...  101 us
    all_gather x1, waiting for transfers between devices, on_device(): row_block = lax.all_gather(arrived, 'dp', axis=0, tiled=True)  39.8 us
    all_to_all x1, blocking collectives, on_device(): lax.all_to_all(outgoing, 'expert', split_axis=0, concat_axis=0, tiled=True)  32.9 us
    all_gather x1, blocking collectives, on_device(): full_rows = lax.all_gather(tokens, 'tensor', axis=1, tiled=True)  19.7 us
    all_to_all x1, starting transfers between devices, on_device(): lax.all_to_all(summed, 'expert', split_axis=0, concat_axis=0, tiled=True)  12 us
    all_to_all x1, waiting for transfers between devices, on_device(): lax.all_to_all(summed, 'expert', split_axis=0, concat_axis=0, tiled=True)  11.5 us
  transfers between devices with their start and end apart: 3, of which 3 were waited for; matrix products, arithmetic and copies ran while one was open for 0% of the time, Pallas kernels for 0%

commit v1 on v0

v1 whole, which is shorter than its diff:
```python
import jax
import jax.numpy as jnp
from jax import lax
from jax.experimental import pallas as pl
from jax.experimental.pallas import tpu as pltpu
from jax.sharding import PartitionSpec as P

MESH = pl.DeviceIdType.MESH
BF16 = jnp.bfloat16
F32 = jnp.float32
NX, NZ, NY = 4, 16, 4
CHUNKS = ((0, 1, -1, 2, -2, 3, -3, 4), (-4, 5, -5, 6, -6, 7, -7, 8))
NCH = len(CHUNKS)
SLOTS = 4
LANES = 128
FAR_FIRST = (2, 1, 3)


def iota(shape, dim):
    return lax.broadcasted_iota(jnp.int32, shape, dim)


def unfold_matrix(count, transposed):
    size = 16 * count
    row, col = iota((size, size), 0), iota((size, size), 1)
    if transposed:
        row, col = col, row
    wanted = (row % (SLOTS * count)) // SLOTS * 16 + row // (SLOTS * count) * SLOTS + row % SLOTS
    return jnp.where(wanted == col, 1.0, 0.0).astype(BF16)


def kernel(tok_hbm, ids_hbm, rw_hbm, wg_hbm, wu_hbm, wd_hbm, out_ref,
           tok, ids, rw, wg, wu, wd, ob, zr, xg, sc, rc, own, s1, r1x, r1y, s2x, s2y, r2x, r2y, fo, rb,
           load_sem, send_sem, z_sem, p1_sem, p2_sem, core_sem, rcore_sem, q1x_sem, q1y_sem, q2x_sem, q2y_sem, back_sem):
    x, z, t = lax.axis_index("dp"), lax.axis_index("expert"), lax.axis_index("tensor")
    y, c = t // 2, t % 2
    per = SLOTS * len(CHUNKS[0])

    def dev(dx=0, dz=0, dy=0, twin=False):
        other = 1 - c if twin else c
        return ((x + dx + NX) % NX, (z + dz + NZ) % NZ, (y + dy) % NY * 2 + other)

    barrier = pltpu.get_barrier_semaphore()
    partners = [dict(dz=d) for d in (8, 7, 9, 6, 10, 5, 11, 4, 12, 3, 13, 2, 14, 1, 15)]
    partners += [dict(dx=d) for d in FAR_FIRST] + [dict(dy=d) for d in FAR_FIRST] + [dict(twin=True)]
    for partner in partners:
        pl.semaphore_signal(barrier, inc=1, device_id=dev(**partner), device_id_type=MESH)

    loads = [
        pltpu.make_async_copy(ids_hbm, ids, load_sem.at[0]),
        pltpu.make_async_copy(rw_hbm, rw, load_sem.at[1]),
        pltpu.make_async_copy(tok_hbm, tok, load_sem.at[2]),
        pltpu.make_async_copy(wg_hbm.at[0], wg, load_sem.at[3]),
        pltpu.make_async_copy(wu_hbm.at[0], wu, load_sem.at[4]),
    ]
    for i in range(8):
        loads.append(pltpu.make_async_copy(wd_hbm.at[0, :, pl.ds(i * 512, 512)], wd.at[i], load_sem.at[5 + i]))
    for load in loads:
        load.start()

    sent = []

    def send(src, dst, sem, device):
        copy = pltpu.make_async_remote_copy(
            src_ref=src, dst_ref=dst, send_sem=send_sem.at[len(sent)], recv_sem=sem,
            device_id=device, device_id_type=MESH)
        copy.start()
        sent.append(copy)

    def arrived(ref, sem):
        pltpu.make_async_copy(ref, ref, sem).wait()

    for load in loads[:3]:
        load.wait()
    shape = (16, 256)
    q = iota(shape, 1)
    hits = [ids[:, k:k + 1] == q // 16 for k in range(3)]
    hit = jnp.where(hits[0] | hits[1] | hits[2], 1.0, 0.0)
    below = jnp.where(iota((16, 16), 0) > iota((16, 16), 1), 1.0, 0.0)
    place = jnp.dot(below.astype(BF16), hit.astype(BF16), preferred_element_type=F32)
    here = place == (q % SLOTS).astype(F32)
    picked = jnp.where(here, hit, 0.0)
    weight = jnp.zeros(shape, F32)
    for k in range(3):
        weight = weight + jnp.where(hits[k] & here, rw[:, k:k + 1], 0.0)
    piece = q // SLOTS % 4
    pick_rows = jnp.concatenate([jnp.where(piece == j, picked, 0.0) for j in range(4)], axis=0).astype(BF16)
    weights = jnp.concatenate([jnp.where(piece == j, weight, 0.0) for j in range(4)], axis=0)
    token_pieces = jnp.concatenate([tok[:, j * LANES:(j + 1) * LANES] for j in range(4)], axis=0)
    slot_rows = lax.dot_general(pick_rows, token_pieces, (((0,), (0,)), ((), ())), preferred_element_type=F32)
    ob[...] = slot_rows.astype(BF16).reshape(16, 16, LANES)
    zr[0] = ob[z]

    pl.semaphore_wait(barrier, len(partners))

    for k in reversed(range(NCH)):
        for i in reversed(range(len(CHUNKS[k]))):
            d = CHUNKS[k][i]
            if d != 0:
                send(ob.at[(z - d + NZ) % NZ], zr.at[k * len(CHUNKS[0]) + i], z_sem.at[k], dev(dz=-d))

    count = len(CHUNKS[0])
    unfold = unfold_matrix(count, False)
    fold = unfold_matrix(count, True)

    def gather_start(k):
        first = k * count
        own_place = 1 if k == 0 else 0
        arrived(zr.at[pl.ds(first + own_place, count - own_place)], z_sem.at[k])
        folded = zr[pl.ds(first, count)].reshape(count * 16, LANES)
        rows = jnp.dot(unfold, folded, preferred_element_type=F32).astype(BF16)
        for j in range(4):
            xg[k, c, y, j // 2, 0, :, (j % 2) * LANES:(j % 2 + 1) * LANES] = rows[j * per:(j + 1) * per]
        for i in FAR_FIRST:
            send(xg.at[k, c, y, 0, 0], xg.at[k, c, y, 0, 4 - i], p1_sem.at[k, 0, i - 1], dev(dx=i))
            send(xg.at[k, c, y, 1, 0], xg.at[k, c, y, 1, 0], p1_sem.at[k, 1, i - 1], dev(dy=i))
        forward(k, 0, 0)
        forward(k, 1, 0)

    def forward(k, h, i):
        if h == 0:
            place = xg.at[k, c, y, 0, (4 - i) % 4]
            if i:
                arrived(place, p1_sem.at[k, 0, i - 1])
            for j in FAR_FIRST:
                send(place, place, p2_sem.at[k, 0, j - 1], dev(dy=j))
        else:
            line = (y - i + 4) % 4
            place = xg.at[k, c, line, 1, 0]
            if i:
                arrived(place, p1_sem.at[k, 1, i - 1])
            for j in FAR_FIRST:
                send(place, xg.at[k, c, line, 1, 4 - j], p2_sem.at[k, 1, j - 1], dev(dx=j))

    def group(k, h, g, core):
        if h == 0:
            return xg.at[k, core, (y - g + 4) % 4, 0]
        return xg.at[k, core, pl.ds(0, 4), 1, (4 - g) % 4]

    def to_twin(k, h, g):
        place = group(k, h, g, c)
        if g:
            arrived(place, p2_sem.at[k, h, g - 1])
        send(place, place, core_sem.at[k, h, g], dev(twin=True))

    def gather_end(k):
        for h in range(2):
            for g in range(4):
                arrived(group(k, h, g, 1 - c), core_sem.at[k, h, g])

    def hidden_of(k):
        gate = up = jnp.zeros((4 * per, 160), F32)
        for core in range(2):
            for line in range(4):
                for h in range(2):
                    left = xg[k, core, line, h].reshape(4 * per, 256)
                    start = (line * 2 + core) * 512 + h * 256
                    dims = (((1,), (1,)), ((), ()))
                    gate = gate + lax.dot_general(left, wg[:, start:start + 256], dims, preferred_element_type=F32)
                    up = up + lax.dot_general(left, wu[:, start:start + 256], dims, preferred_element_type=F32)
        return (gate / (1.0 + jnp.exp(-gate)) * up).astype(BF16)

    def down(k, hidden, j, twin):
        out = jnp.dot(hidden, wd[(y + j) % 4 * 2 + (1 - c if twin else c)], preferred_element_type=F32)
        for h in range(2):
            part = out[:, h * 256:(h + 1) * 256].reshape(4, per, 256)
            if twin:
                sc[k, j, h] = part.astype(BF16)
            else:
                own[k, j, h] = part
        if twin:
            send(sc.at[k, j], rc.at[k, j], rcore_sem.at[k, j], dev(twin=True))

    def sum_cores(k, j):
        arrived(rc.at[k, j], rcore_sem.at[k, j])
        first = own[k, j, 0] + rc[k, j, 0].astype(F32)
        own[k, j, 0, 0] = first[0]
        s1[k, j, 0] = first.astype(BF16)
        for i in FAR_FIRST:
            send(s1.at[k, j, 0, i], r1x.at[k, i - 1, j], q1x_sem.at[k, i - 1], dev(dx=i))
        second = own[k, j, 1] + rc[k, j, 1].astype(F32)
        if j:
            s1[k, j, 1] = second.astype(BF16)
            send(s1.at[k, j, 1], r1y.at[k, j - 1], q1y_sem.at[k, j - 1], dev(dy=j))
        else:
            own[k, 0, 1] = second

    def sum_first(k):
        for i in range(3):
            arrived(r1y.at[k, i], q1y_sem.at[k, i])
        for i in FAR_FIRST + (0,):
            total = own[k, 0, 1, i]
            for n in range(3):
                total = total + r1y[k, n, i].astype(F32)
            if i:
                s2y[k, i - 1] = total.astype(BF16)
                send(s2y.at[k, i - 1], r2y.at[k, i - 1], q2y_sem.at[k, i - 1], dev(dx=i))
            else:
                own[k, 0, 1, 0] = total
        for i in range(3):
            arrived(r1x.at[k, i], q1x_sem.at[k, i])
        for j in FAR_FIRST + (0,):
            total = own[k, j, 0, 0]
            for n in range(3):
                total = total + r1x[k, n, j].astype(F32)
            if j:
                s2x[k, j - 1] = total.astype(BF16)
                send(s2x.at[k, j - 1], r2x.at[k, j - 1], q2x_sem.at[k, j - 1], dev(dy=j))
            else:
                own[k, 0, 0, 0] = total

    def send_back(k):
        pieces = []
        for h, landed, sem in ((0, r2x, q2x_sem), (1, r2y, q2y_sem)):
            total = own[k, 0, h, 0]
            for n in range(3):
                arrived(landed.at[k, n], sem.at[k, n])
                total = total + landed[k, n].astype(F32)
            total = total.astype(BF16)
            pieces += [total[:, :LANES], total[:, LANES:]]
        rows = jnp.dot(fold, jnp.concatenate(pieces, axis=0), preferred_element_type=F32).astype(BF16)
        fo[pl.ds(k * count, count)] = rows.reshape(count, 16, LANES)
        for i in reversed(range(count)):
            d = CHUNKS[k][i]
            if d:
                send(fo.at[k * count + i], rb.at[z], back_sem.at[0], dev(dz=d))
            else:
                rb[z] = fo[k * count + i]

    schedule(gather_start, forward, to_twin, gather_end, hidden_of, down, sum_cores, sum_first, send_back, loads)

    arrived(rb.at[pl.ds(0, NZ - 1)], back_sem.at[0])
    high = weights.astype(BF16)
    rest = weights - high.astype(F32)
    middle = rest.astype(BF16)
    low = (rest - middle.astype(F32)).astype(BF16)
    stacked = jnp.concatenate([high, middle, low], axis=0)
    mixed = jnp.dot(stacked, rb[...].reshape(256, LANES), preferred_element_type=F32)
    mixed = mixed[:64] + mixed[64:128] + mixed[128:]
    for j in range(4):
        out_ref[:, j * LANES:(j + 1) * LANES] = mixed[j * 16:(j + 1) * 16].astype(BF16)
    for copy in sent:
        copy.wait_send()


def schedule(gather_start, forward, to_twin, gather_end, hidden_of, down, sum_cores, sum_first, send_back, loads):
    def hand_on(k):
        for i in (1, 3, 2):
            for h in range(2):
                forward(k, h, i)
        for h in range(2):
            to_twin(k, h, 0)

    def hand_over(k):
        for g in (1, 3, 2):
            for h in range(2):
                to_twin(k, h, g)

    def multiply(k):
        hidden = hidden_of(k)
        for twin in (True, False):
            for j in FAR_FIRST + (0,):
                down(k, hidden, j, twin)

    def spread(k):
        for j in FAR_FIRST + (0,):
            sum_cores(k, j)

    gather_start(0)
    hand_on(0)
    gather_start(1)
    hand_over(0)
    hand_on(1)
    for load in loads[3:]:
        load.wait()
    gather_end(0)
    multiply(0)
    hand_over(1)
    spread(0)
    gather_end(1)
    multiply(1)
    sum_first(0)
    spread(1)
    send_back(0)
    sum_first(1)
    send_back(1)


def on_device(*args):
    per = SLOTS * len(CHUNKS[0])
    dma = lambda *shape: pltpu.SemaphoreType.DMA(shape)
    vmem = pltpu.VMEM
    return pl.pallas_call(
        kernel,
        out_shape=jax.ShapeDtypeStruct((16, 512), BF16),
        in_specs=[pl.BlockSpec(memory_space=pl.ANY)] * 6,
        out_specs=pl.BlockSpec(memory_space=pltpu.VMEM),
        scratch_shapes=[
            vmem((16, 512), BF16), vmem((16, 3), jnp.int32), vmem((16, 3), F32),
            vmem((160, 4096), BF16), vmem((160, 4096), BF16), vmem((8, 160, 512), BF16),
            vmem((16, 16, LANES), BF16), vmem((16, 16, LANES), BF16),
            vmem((NCH, 2, 4, 2, 4, per, 256), BF16),
            vmem((NCH, 4, 2, 4, per, 256), BF16), vmem((NCH, 4, 2, 4, per, 256), BF16),
            vmem((NCH, 4, 2, 4, per, 256), F32),
            vmem((NCH, 4, 2, 4, per, 256), BF16),
            vmem((NCH, 3, 4, per, 256), BF16), vmem((NCH, 3, 4, per, 256), BF16),
            vmem((NCH, 3, per, 256), BF16), vmem((NCH, 3, per, 256), BF16),
            vmem((NCH, 3, per, 256), BF16), vmem((NCH, 3, per, 256), BF16),
            vmem((16, 16, LANES), BF16), vmem((16, 16, LANES), BF16),
            dma(13), dma(30 + NCH * 63), dma(NCH),
            dma(NCH, 2, 3), dma(NCH, 2, 3), dma(NCH, 2, 4), dma(NCH, 4),
            dma(NCH, 3), dma(NCH, 3), dma(NCH, 3), dma(NCH, 3), dma(1),
        ],
        compiler_params=pltpu.CompilerParams(
            collective_id=0, has_side_effects=True, vmem_limit_bytes=40 << 20),
        name="experts",
    )(*args)


def solution(mesh):
    placed = (
        P(("dp", "expert"), "tensor"),
        P(("dp", "expert"), None),
        P(("dp", "expert"), None),
        P("expert", ("dp", "tensor"), None),
        P("expert", ("dp", "tensor"), None),
        P("expert", ("dp", "tensor"), None),
    )
    return jax.shard_map(
        on_device,
        mesh=mesh,
        in_specs=placed,
        out_specs=P(("dp", "expert"), "tensor"),
        check_vma=False,
    )
```

time: 244 us -> 63 us (0.26)
  the two profiles are of different devices: /device:TPU:1 before, /device:TPU:8 now
where the time goes in v1:
time: 63 us; the launch traced here: 62.7 us
  Pallas kernels  55.9 us (89%)
  local copies, waits for them, and re-layouts  6.79 us (11%)
    pallas_call x1, Pallas kernels, on_device(): pl.pallas_call(kernel, out_shape=jax.ShapeDtypeStruct((16, 512), BF16), i...  55.9 us
    unnamed x11, local copies, waits for them, and re-layouts  6.79 us

profile of v1, /device:TPU:8, one launch (start us, length us, event | category | flops | bytes accessed | tf_op | source)
XLA Modules:
  0.0 62.7 jit_solution(2264858140740355810)
XLA Ops:
  0.0 0.8 %copy.7.ids_hbm = s32[16,3]{1,0:T(8,128)S(1)} copy(s32[16,3]{0,1:T(4,128)} %param.7) | data formatting | bytes 384 | tf_op args[1]
  0.8 0.8 %copy.8.rw_hbm = f32[16,3]{1,0:T(8,128)S(1)} copy(f32[16,3]{0,1:T(4,128)} %param.8) | data formatting | bytes 384 | tf_op args[2]
  1.5 0.0 copy-start
  1.5 1.3 %copy-done = bf16[1,160,4096]{2,1,0:T(8,128)(2,1)S(1)} copy-done((bf16[1,160,4096]{2,1,0:T(8,128)(2,1)S(1)}, bf16[1,160,4096]{2,1,0:T(8,128)(2,1)}, u32[]{:S(2)}) %copy-start) | copy-done | bytes 1310744
  2.8 0.0 copy-start.1
  2.8 1.3 %copy-done.1 = bf16[1,160,4096]{2,1,0:T(8,128)(2,1)S(1)} copy-done((bf16[1,160,4096]{2,1,0:T(8,128)(2,1)S(1)}, bf16[1,160,4096]{2,1,0:T(8,128)(2,1)}, u32[]{:S(2)}) %copy-start.1) | copy-done | bytes 1310744
  4.2 0.0 copy-start.2
  4.2 1.3 %copy-done.2 = bf16[1,160,4096]{2,1,0:T(8,128)(2,1)S(1)} copy-done((bf16[1,160,4096]{2,1,0:T(8,128)(2,1)S(1)}, bf16[1,160,4096]{2,1,0:T(8,128)(2,1)}, u32[]{:S(2)}) %copy-start.2) | copy-done | bytes 1310744
  5.5 0.0 copy-start.3
  5.5 0.7 %copy-done.3 = bf16[16,512]{1,0:T(8,128)(2,1)S(1)} copy-done((bf16[16,512]{1,0:T(8,128)(2,1)S(1)}, bf16[16,512]{1,0:T(8,128)(2,1)}, u32[]{:S(2)}) %copy-start.3) | copy-done | bytes 16408
  6.2 55.9 %experts.1 = bf16[16,512]{1,0:T(8,128)(2,1)S(1)} custom-call(bf16[16,512]{1,0:T(8,128)(2,1)S(1)} %copy-done.3, s32[16,3]{1,0:T(8,128)S(1)} %copy.7.ids_hbm, f32[16,3]{1,0:T(8,128)S(1)} %copy.8.rw_hbm, bf16[1,160,4096]{2,1,0:T(8,128)(2,1)S(1)} %copy-done, bf16[1,160,4096]{2,1,0:T(8,128)(2,1)S(1)} %copy-done.1, bf16[1,160,4096]{2,1,0:T(8,128)(2,1)S(1)} %copy-done.2), custom_call_target="tpu_custom_call" | custom-call | tf_op jit(solution)/shard_map/experts/pallas_call | solution.py:293
  62.1 0.6 copy.10
Async XLA Ops:
  1.5 1.3 %copy-start = (bf16[1,160,4096]{2,1,0:T(8,128)(2,1)S(1)}, bf16[1,160,4096]{2,1,0:T(8,128)(2,1)}, u32[]{:S(2)}) copy-start(bf16[1,160,4096]{2,1,0:T(8,128)(2,1)} %wg_hbm.1) | copy-start | bytes 3932164
  2.8 1.3 %copy-start.1 = (bf16[1,160,4096]{2,1,0:T(8,128)(2,1)S(1)}, bf16[1,160,4096]{2,1,0:T(8,128)(2,1)}, u32[]{:S(2)}) copy-start(bf16[1,160,4096]{2,1,0:T(8,128)(2,1)} %wu_hbm.1) | copy-start | bytes 3932164
  4.2 1.3 %copy-start.2 = (bf16[1,160,4096]{2,1,0:T(8,128)(2,1)S(1)}, bf16[1,160,4096]{2,1,0:T(8,128)(2,1)}, u32[]{:S(2)}) copy-start(bf16[1,160,4096]{2,1,0:T(8,128)(2,1)} %wd_hbm.1) | copy-start | bytes 3932164
  5.5 0.7 %copy-start.3 = (bf16[16,512]{1,0:T(8,128)(2,1)S(1)}, bf16[16,512]{1,0:T(8,128)(2,1)}, u32[]{:S(2)}) copy-start(bf16[16,512]{1,0:T(8,128)(2,1)} %tok_hbm.1) | copy-start | bytes 49156

commit v2 on v0

v2 whole, which is shorter than its diff:
```python
import jax
import jax.numpy as jnp
from jax import lax
from jax.experimental import pallas as pl
from jax.experimental.pallas import tpu as pltpu
from jax.sharding import PartitionSpec as P

MESH = pl.DeviceIdType.MESH
BF16 = jnp.bfloat16
F32 = jnp.float32
NZ = 16
SLOTS = 4
LANES = 128
PIECES = 4
HID = 160
COUNT = 4
ROWS = COUNT * SLOTS
FAR_FIRST = (2, 1, 3)
IN_ORDER = (0, 1, 3, 2)


def iota(shape, dim):
    return lax.broadcasted_iota(jnp.int32, shape, dim)


def source_of(core, k, i):
    return 4 * k + i - core * (4 + 8 * k)


def place_of(expert):
    source = (8 - expert) % NZ - 8
    if source >= 0:
        return 0, source // 4, source % 4
    return 1, int(source < -4), source % 4


def unfold_matrix(transposed):
    size = 16 * COUNT
    row, col = iota((size, size), 0), iota((size, size), 1)
    if transposed:
        row, col = col, row
    wanted = (row % ROWS) // SLOTS * 16 + row // ROWS * SLOTS + row % SLOTS
    return jnp.where(wanted == col, 1.0, 0.0).astype(BF16)


def kernel(tok_hbm, ids_hbm, rw_hbm, wg_hbm, wu_hbm, wd_hbm, out_ref,
           tok, ids, rw, wg, wu, wd, ob, mix, up_held, down_held, zr, xg, own0, own1, s1x, s1y, r1x, r1y, s2x, s2y, r2x, r2y, fo, rb,
           load_sem, twin_sem, twin_send, send_sem, self_send, z_sem, hold_sem, p1_sem, p2_sem, q1x_sem, q1y_sem, q2x_sem, q2y_sem,
           back_sem):
    x, z, t = lax.axis_index("dp"), lax.axis_index("expert"), lax.axis_index("tensor")
    y, c = t // 2, t % 2

    def dev(dx=0, dz=0, dy=0, core=c):
        return ((x + dx + 4) % 4, (z + dz + NZ) % NZ, (y + dy) % 4 * 2 + core)

    barrier = pltpu.get_barrier_semaphore()
    loads = [
        pltpu.make_async_copy(ids_hbm, ids, load_sem.at[0]),
        pltpu.make_async_copy(rw_hbm, rw, load_sem.at[1]),
        pltpu.make_async_copy(tok_hbm, tok, load_sem.at[2]),
        pltpu.make_async_copy(wg_hbm.at[0], wg.at[pl.ds(0, HID)], load_sem.at[3]),
        pltpu.make_async_copy(wu_hbm.at[0], wu.at[pl.ds(0, HID)], load_sem.at[4]),
    ]
    for i in range(8):
        loads.append(pltpu.make_async_copy(wd_hbm.at[0, :, pl.ds(i * 512, 512)], wd.at[i, pl.ds(0, HID)], load_sem.at[5 + i]))
    for load in loads[:3]:
        load.start()
    partners = [dict(dz=d, core=core) for d in (4, -4, 3, -3, 2, -2, 1, -1) for core in range(2)]
    partners += [dict(dx=d) for d in FAR_FIRST] + [dict(dy=d) for d in FAR_FIRST] + [dict(core=1 - c)]
    for partner in partners:
        pl.semaphore_signal(barrier, inc=1, device_id=dev(**partner), device_id_type=MESH)
    for load in loads[3:]:
        load.start()

    sent = []

    def send(src, dst, sem, device):
        copy = pltpu.make_async_remote_copy(
            src_ref=src, dst_ref=dst, send_sem=send_sem.at[len(sent)], recv_sem=sem,
            device_id=device, device_id_type=MESH)
        copy.start()
        sent.append(copy)

    def arrived(ref, sem):
        pltpu.make_async_copy(ref, ref, sem).wait()

    for load in loads[:3]:
        load.wait()
    shape = (256, 64)
    q, lane = iota(shape, 0), iota(shape, 1)
    steps_up = (ids[...] - z + NZ) % NZ
    ids_wide = jnp.concatenate([steps_up] * PIECES, axis=1)
    rw_wide = jnp.concatenate([rw[...]] * PIECES, axis=1)
    hits = [ids_wide[k:k + 1] == q // 16 for k in range(3)]
    hit = jnp.where(hits[0] | hits[1] | hits[2], 1.0, 0.0)
    source, row = iota((64, 64), 0), iota((64, 64), 1)
    below = jnp.where((source // 16 == row // 16) & (source < row), 1.0, 0.0)
    place = jnp.dot(hit.astype(BF16), below.astype(BF16), preferred_element_type=F32)
    here = (place == (q % SLOTS).astype(F32)) & (q // SLOTS % PIECES == lane // 16)
    picked = jnp.where(here, hit, 0.0).astype(BF16)
    weights = jnp.zeros(shape, F32)
    for k in range(3):
        weights = weights + jnp.where(hits[k] & here, rw_wide[k:k + 1], 0.0)
    token_pieces = jnp.concatenate([tok[:, j * LANES:(j + 1) * LANES] for j in range(PIECES)], axis=0)
    slot_rows = jnp.dot(picked, token_pieces, preferred_element_type=F32)
    ob[...] = slot_rows.astype(BF16).reshape(16, 16, LANES)
    unfold = unfold_matrix(False)
    fold = unfold_matrix(True)

    pl.semaphore_wait(barrier, len(partners))

    send(ob.at[pl.ds(5, 4)], up_held, hold_sem.at[0], dev(dz=4))
    send(ob.at[pl.ds(9, 3)], down_held, hold_sem.at[1], dev(dz=-4))
    for d in (4, -4, 3, -3, 2, -2, 1, -1):
        core, k, i = place_of(d)
        send(ob.at[d % NZ], zr.at[k, c, i], z_sem.at[k], dev(dz=d, core=core))
    to_self = pltpu.make_async_copy(ob.at[0], zr.at[0, 0, 0], z_sem.at[0])
    to_near = pltpu.make_async_remote_copy(
        src_ref=ob.at[0], dst_ref=zr.at[0, 1, 0], send_sem=self_send.at[0], recv_sem=z_sem.at[0],
        device_id=dev(core=0), device_id_type=MESH)
    pl.when(c == 0)(to_self.start)
    pl.when(c == 1)(to_near.start)

    to_twin = []

    def twin(src, dst):
        n = len(to_twin)
        copy = pltpu.make_async_remote_copy(
            src_ref=src, dst_ref=dst, send_sem=twin_send.at[n], recv_sem=twin_sem.at[n],
            device_id=dev(core=1 - c), device_id_type=MESH)
        copy.start()
        to_twin.append(copy)

    twin(wg_hbm.at[0], wg.at[pl.ds(HID, HID)])
    twin(wu_hbm.at[0], wu.at[pl.ds(HID, HID)])
    for i in range(8):
        twin(wd_hbm.at[0, :, pl.ds(i * 512, 512)], wd.at[i, pl.ds(HID, HID)])

    by_row = weights.T
    high = by_row.astype(BF16)
    rest = by_row - high.astype(F32)
    middle = rest.astype(BF16)
    mix[0:64] = high
    mix[64:128] = middle
    mix[128:192] = (rest - middle.astype(F32)).astype(BF16)

    arrived(up_held, hold_sem.at[0])
    for n in range(4):
        core, k, i = place_of(5 + n)
        send(up_held.at[n], zr.at[k, c, i], z_sem.at[k], dev(dz=1 + n, core=core))
    arrived(down_held, hold_sem.at[1])
    for n in range(3):
        core, k, i = place_of(9 + n)
        send(down_held.at[n], zr.at[k, c, i], z_sem.at[k], dev(dz=n - 3, core=core))

    def forward(k, h, i):
        if h == 0:
            place = xg.at[k, 0, y, (4 - i) % 4]
            if i:
                arrived(place, p1_sem.at[k, 0, i - 1])
            for j in FAR_FIRST:
                send(place, place, p2_sem.at[k, 0, j - 1], dev(dy=j))
        else:
            line = (y - i + 4) % 4
            place = xg.at[k, 1, line, 0]
            if i:
                arrived(place, p1_sem.at[k, 1, i - 1])
            for j in FAR_FIRST:
                send(place, xg.at[k, 1, line, 4 - j], p2_sem.at[k, 1, j - 1], dev(dx=j))

    def gather_start(k):
        arrived(zr.at[k], z_sem.at[k])
        for h in range(2):
            rows = jnp.dot(unfold, zr[k, h].reshape(COUNT * 16, LANES), preferred_element_type=F32).astype(BF16)
            for j in range(PIECES):
                xg[k, h, y, 0, :, j * LANES:(j + 1) * LANES] = rows[j * ROWS:(j + 1) * ROWS]
            for i in FAR_FIRST:
                if h == 0:
                    send(xg.at[k, 0, y, 0], xg.at[k, 0, y, 4 - i], p1_sem.at[k, 0, i - 1], dev(dx=i))
                else:
                    send(xg.at[k, 1, y, 0], xg.at[k, 1, y, 0], p1_sem.at[k, 1, i - 1], dev(dy=i))
        for h in range(2):
            forward(k, h, 0)

    def hand_on(k):
        for i in IN_ORDER[1:]:
            for h in range(2):
                forward(k, h, i)

    def gather_end(k):
        for j in IN_ORDER[1:]:
            arrived(xg.at[k, 0, (y - j + 4) % 4], p2_sem.at[k, 0, j - 1])
            arrived(xg.at[k, 1, pl.ds(0, 4), 4 - j], p2_sem.at[k, 1, j - 1])

    def hidden_of(k):
        gate = up = jnp.zeros((4 * ROWS, 2 * HID), F32)
        for h in range(2):
            for line in range(4):
                left = xg[k, h, line].reshape(4 * ROWS, 512)
                start = (line * 2 + h) * 512
                dims = (((1,), (1,)), ((), ()))
                gate = gate + lax.dot_general(left, wg[:, start:start + 512], dims, preferred_element_type=F32)
                up = up + lax.dot_general(left, wu[:, start:start + 512], dims, preferred_element_type=F32)
        return (gate / (1.0 + jnp.exp(-gate)) * up).astype(BF16)

    def spread(k, hidden):
        for j in FAR_FIRST + (0,):
            for h in range(2):
                out = jnp.dot(hidden, wd[(y + j) % 4 * 2 + h], preferred_element_type=F32).reshape(4, ROWS, 512)
                if h == 0:
                    own0[k, j] = out[0]
                    s1x[k, j] = out[1:].astype(BF16)
                    for i in FAR_FIRST:
                        send(s1x.at[k, j, i - 1], r1x.at[k, i - 1, j], q1x_sem.at[k, i - 1], dev(dx=i))
                elif j:
                    s1y[k, j - 1] = out.astype(BF16)
                    send(s1y.at[k, j - 1], r1y.at[k, j - 1], q1y_sem.at[k, j - 1], dev(dy=j))
                else:
                    own1[k] = out

    def sum_first(k):
        for n in range(3):
            arrived(r1y.at[k, n], q1y_sem.at[k, n])
        for i in FAR_FIRST + (0,):
            total = own1[k, i]
            for n in range(3):
                total = total + r1y[k, n, i].astype(F32)
            if i:
                s2y[k, i - 1] = total.astype(BF16)
                send(s2y.at[k, i - 1], r2y.at[k, i - 1], q2y_sem.at[k, i - 1], dev(dx=i))
            else:
                own1[k, 0] = total
        for n in range(3):
            arrived(r1x.at[k, n], q1x_sem.at[k, n])
        for j in FAR_FIRST + (0,):
            total = own0[k, j]
            for n in range(3):
                total = total + r1x[k, n, j].astype(F32)
            if j:
                s2x[k, j - 1] = total.astype(BF16)
                send(s2x.at[k, j - 1], r2x.at[k, j - 1], q2x_sem.at[k, j - 1], dev(dy=j))
            else:
                own0[k, 0] = total

    def send_back(k):
        for h, own, landed, sem in ((1, own1, r2y, q2y_sem), (0, own0, r2x, q2x_sem)):
            total = own[k, 0]
            for n in range(3):
                arrived(landed.at[k, n], sem.at[k, n])
                total = total + landed[k, n].astype(F32)
            total = total.astype(BF16)
            pieces = [total[:, j * LANES:(j + 1) * LANES] for j in range(PIECES)]
            rows = jnp.dot(fold, jnp.concatenate(pieces, axis=0), preferred_element_type=F32).astype(BF16)
            fo[k, h] = rows.reshape(COUNT, 16, LANES)
            for i in reversed(range(COUNT)):
                d = source_of(c, k, i)
                if k or i:
                    send(fo.at[k, h, i], rb.at[(NZ - d) % NZ], back_sem.at[0], dev(dz=d, core=h))
                elif h:
                    send(fo.at[0, 1, 0], rb.at[4 * c], back_sem.at[1 - c], dev(dz=d, core=1))
                else:
                    pl.when(c == 0)(back_self.start)
                    pl.when(c == 1)(back_near.start)

    back_self = pltpu.make_async_copy(fo.at[0, 0, 0], rb.at[0], back_sem.at[1])
    back_near = pltpu.make_async_remote_copy(
        src_ref=fo.at[0, 0, 0], dst_ref=rb.at[4], send_sem=self_send.at[1], recv_sem=back_sem.at[0],
        device_id=dev(dz=-4, core=0), device_id_type=MESH)

    gather_start(0)
    hand_on(0)
    gather_start(1)
    hand_on(1)
    for load in loads[3:]:
        load.wait()
    for copy in to_twin:
        copy.wait_recv()
    gather_end(0)
    spread(0, hidden_of(0))
    gather_end(1)
    spread(1, hidden_of(1))
    sum_first(0)
    sum_first(1)
    send_back(0)
    send_back(1)

    arrived(rb.at[0], back_sem.at[1])
    arrived(rb.at[pl.ds(1, NZ - 1)], back_sem.at[0])
    terms = jnp.dot(mix[...], rb[...].reshape(256, LANES), preferred_element_type=F32)
    mixed = terms[:64] + terms[64:128] + terms[128:]
    for j in range(PIECES):
        out_ref[:, j * LANES:(j + 1) * LANES] = mixed[j * 16:(j + 1) * 16].astype(BF16)

    for copy in sent + to_twin:
        copy.wait_send()
    pl.when(c == 1)(to_near.wait_send)
    pl.when(c == 1)(back_near.wait_send)


def on_device(tokens, expert_ids, route_weights, gate_weight, up_weight, down_weight):
    dma = lambda *shape: pltpu.SemaphoreType.DMA(shape)
    vmem = pltpu.VMEM
    return pl.pallas_call(
        kernel,
        out_shape=jax.ShapeDtypeStruct((16, 512), BF16),
        in_specs=[pl.BlockSpec(memory_space=pltpu.HBM)] * 6,
        out_specs=pl.BlockSpec(memory_space=pltpu.VMEM),
        scratch_shapes=[
            vmem((16, 512), BF16), vmem((3, 16), jnp.int32), vmem((3, 16), F32),
            vmem((2 * HID, 4096), BF16), vmem((2 * HID, 4096), BF16), vmem((8, 2 * HID, 512), BF16),
            vmem((16, 16, LANES), BF16), vmem((192, 256), BF16),
            vmem((4, 16, LANES), BF16), vmem((3, 16, LANES), BF16),
            vmem((2, 2, COUNT, 16, LANES), BF16),
            vmem((2, 2, 4, 4, ROWS, 512), BF16),
            vmem((2, 4, ROWS, 512), F32), vmem((2, 4, ROWS, 512), F32),
            vmem((2, 4, 3, ROWS, 512), BF16), vmem((2, 3, 4, ROWS, 512), BF16),
            vmem((2, 3, 4, ROWS, 512), BF16), vmem((2, 3, 4, ROWS, 512), BF16),
            vmem((2, 3, ROWS, 512), BF16), vmem((2, 3, ROWS, 512), BF16),
            vmem((2, 3, ROWS, 512), BF16), vmem((2, 3, ROWS, 512), BF16),
            vmem((2, 2, COUNT, 16, LANES), BF16), vmem((16, 16, LANES), BF16),
            dma(13), dma(10), dma(10), dma(160), dma(2), dma(2), dma(2), dma(2, 2, 3), dma(2, 2, 3),
            dma(2, 3), dma(2, 3), dma(2, 3), dma(2, 3), dma(2),
        ],
        compiler_params=pltpu.CompilerParams(
            collective_id=0, has_side_effects=True, vmem_limit_bytes=60 << 20),
        name="experts",
    )(tokens, expert_ids.T, route_weights.T, gate_weight, up_weight, down_weight)


def solution(mesh):
    placed = (
        P(("dp", "expert"), "tensor"),
        P(("dp", "expert"), None),
        P(("dp", "expert"), None),
        P("expert", ("dp", "tensor"), None),
        P("expert", ("dp", "tensor"), None),
        P("expert", ("dp", "tensor"), None),
    )
    return jax.shard_map(
        on_device,
        mesh=mesh,
        in_specs=placed,
        out_specs=P(("dp", "expert"), "tensor"),
        check_vma=False,
    )
```

time: 244 us -> 56.3 us (0.23)
  waiting for transfers between devices: 152 us -> 0 us
  Pallas kernels: 0 us -> 54.8 us
  blocking collectives: 52.5 us -> 0 us
  between operations: 13.5 us -> 0.01 us
  starting transfers between devices: 12 us -> 0 us
  matrix products: 5.38 us -> 0 us
  local copies, waits for them, and re-layouts: 5.32 us -> 1.32 us
    reduce_scatter x1 -> x0, waiting for transfers between devices: 101 us -> none  [on_device(): lax.psum_scatter(terms.reshape(slots, -1).astype(jnp.bfloat16), ('dp', 't...]
    pallas_call x0 -> x1, Pallas kernels: none -> 54.8 us  [on_device(): pl.pallas_call(kernel, out_shape=jax.ShapeDtypeStruct((16, 512), BF16), i...]
    all_gather x1 -> x0, waiting for transfers between devices: 39.8 us -> none  [on_device(): row_block = lax.all_gather(arrived, 'dp', axis=0, tiled=True)]
    all_to_all x1 -> x0, blocking collectives: 32.9 us -> none  [on_device(): lax.all_to_all(outgoing, 'expert', split_axis=0, concat_axis=0, tiled=True)]
    all_gather x1 -> x0, blocking collectives: 19.7 us -> none  [on_device(): full_rows = lax.all_gather(tokens, 'tensor', axis=1, tiled=True)]
    all_to_all x1 -> x0, starting transfers between devices: 12 us -> none  [on_device(): lax.all_to_all(summed, 'expert', split_axis=0, concat_axis=0, tiled=True)]
    all_to_all x1 -> x0, waiting for transfers between devices: 11.5 us -> none  [on_device(): lax.all_to_all(summed, 'expert', split_axis=0, concat_axis=0, tiled=True)]
    dot_general x6 -> x0, matrix products: 5.38 us -> none  [the longest x1 2.59 us: on_device(): lax.dot_general(row_block, gate_weight[0], dims, preferred_element_type=j...]
  transfers between devices with their start and end apart: 3 -> 0, of which waited for: 3 -> 0; matrix products, arithmetic and copies ran while one was open for 0% -> 0% of each run, Pallas kernels for 0% -> 0%
where the time goes in v2:
time: 56.3 us; the launch traced here: 56.1 us
  Pallas kernels  54.8 us (97%)
  local copies, waits for them, and re-layouts  1.32 us (2%)
    pallas_call x1, Pallas kernels, on_device(): pl.pallas_call(kernel, out_shape=jax.ShapeDtypeStruct((16, 512), BF16), i...  54.8 us
    unnamed x1, local copies, waits for them, and re-layouts  1.32 us

profile of v2, /device:TPU:1, one launch (start us, length us, event | category | flops | bytes accessed | tf_op | source)
XLA Modules:
  0.0 56.1 jit_solution(15277477117648787684)
XLA Ops:
  0.0 54.8 %experts.1 = bf16[16,512]{1,0:T(8,128)(2,1)} custom-call(bf16[16,512]{1,0:T(8,128)(2,1)} %tok_hbm.1, s32[3,16]{1,0:T(4,128)} %bitcast.2, f32[3,16]{1,0:T(4,128)} %bitcast.3, bf16[1,160,4096]{2,1,0:T(8,128)(2,1)} %wg_hbm.1, bf16[1,160,4096]{2,1,0:T(8,128)(2,1)} %wu_hbm.1, bf16[1,160,4096]{2,1,0:T(8,128)(2,1)} %wd_hbm.1), custom_call_target="tpu_custom_call" | custom-call | tf_op jit(solution)/shard_map/experts/pallas_call | solution.py:303
  54.8 1.3 %copy.8 = bf16[16,512]{1,0:T(8,128)(2,1)} copy(bf16[16,512]{1,0:T(8,128)(2,1)} %experts.1) | data formatting | bytes 32768

commit v3 on v2

--- a/solution.py
+++ b/solution.py
@@ -13,10 +13,12 @@
 LANES = 128
 PIECES = 4
 HID = 160
+UP = 384
 COUNT = 4
 ROWS = COUNT * SLOTS
 FAR_FIRST = (2, 1, 3)
 IN_ORDER = (0, 1, 3, 2)
+LATER = (8, 9, 7, 10, 6, 11, 5)
 
 
 def iota(shape, dim):
@@ -44,7 +46,7 @@
 
 
 def kernel(tok_hbm, ids_hbm, rw_hbm, wg_hbm, wu_hbm, wd_hbm, out_ref,
-           tok, ids, rw, wg, wu, wd, ob, mix, up_held, down_held, zr, xg, own0, own1, s1x, s1y, r1x, r1y, s2x, s2y, r2x, r2y, fo, rb,
+           tok, ids, rw, wgu, wd, ob, mix, held, zr, xg, own0, own1, s1x, s1y, r1x, r1y, s2x, s2y, r2x, r2y, fo, rb,
            load_sem, twin_sem, twin_send, send_sem, self_send, z_sem, hold_sem, p1_sem, p2_sem, q1x_sem, q1y_sem, q2x_sem, q2y_sem,
            back_sem):
     x, z, t = lax.axis_index("dp"), lax.axis_index("expert"), lax.axis_index("tensor")
@@ -58,8 +60,8 @@
         pltpu.make_async_copy(ids_hbm, ids, load_sem.at[0]),
         pltpu.make_async_copy(rw_hbm, rw, load_sem.at[1]),
         pltpu.make_async_copy(tok_hbm, tok, load_sem.at[2]),
-        pltpu.make_async_copy(wg_hbm.at[0], wg.at[pl.ds(0, HID)], load_sem.at[3]),
-        pltpu.make_async_copy(wu_hbm.at[0], wu.at[pl.ds(0, HID)], load_sem.at[4]),
+        pltpu.make_async_copy(wg_hbm.at[0], wgu.at[pl.ds(0, HID)], load_sem.at[3]),
+        pltpu.make_async_copy(wu_hbm.at[0], wgu.at[pl.ds(UP, HID)], load_sem.at[4]),
     ]
     for i in range(8):
         loads.append(pltpu.make_async_copy(wd_hbm.at[0, :, pl.ds(i * 512, 512)], wd.at[i, pl.ds(0, HID)], load_sem.at[5 + i]))
@@ -109,8 +111,8 @@
 
     pl.semaphore_wait(barrier, len(partners))
 
-    send(ob.at[pl.ds(5, 4)], up_held, hold_sem.at[0], dev(dz=4))
-    send(ob.at[pl.ds(9, 3)], down_held, hold_sem.at[1], dev(dz=-4))
+    send(ob.at[pl.ds(5, 4)], held.at[pl.ds(0, 4)], hold_sem.at[0], dev(dz=4))
+    send(ob.at[pl.ds(9, 3)], held.at[pl.ds(4, 3)], hold_sem.at[1], dev(dz=-4))
     for d in (4, -4, 3, -3, 2, -2, 1, -1):
         core, k, i = place_of(d)
         send(ob.at[d % NZ], zr.at[k, c, i], z_sem.at[k], dev(dz=d, core=core))
@@ -131,11 +133,12 @@
         copy.start()
         to_twin.append(copy)
 
-    twin(wg_hbm.at[0], wg.at[pl.ds(HID, HID)])
-    twin(wu_hbm.at[0], wu.at[pl.ds(HID, HID)])
+    twin(wg_hbm.at[0], wgu.at[pl.ds(HID, HID)])
+    twin(wu_hbm.at[0], wgu.at[pl.ds(UP + HID, HID)])
     for i in range(8):
         twin(wd_hbm.at[0, :, pl.ds(i * 512, 512)], wd.at[i, pl.ds(HID, HID)])
 
+    wgu[2 * HID:UP] = jnp.zeros((UP - 2 * HID, 4096), BF16)
     by_row = weights.T
     high = by_row.astype(BF16)
     rest = by_row - high.astype(F32)
@@ -144,14 +147,11 @@
     mix[64:128] = middle
     mix[128:192] = (rest - middle.astype(F32)).astype(BF16)
 
-    arrived(up_held, hold_sem.at[0])
-    for n in range(4):
-        core, k, i = place_of(5 + n)
-        send(up_held.at[n], zr.at[k, c, i], z_sem.at[k], dev(dz=1 + n, core=core))
-    arrived(down_held, hold_sem.at[1])
-    for n in range(3):
-        core, k, i = place_of(9 + n)
-        send(down_held.at[n], zr.at[k, c, i], z_sem.at[k], dev(dz=n - 3, core=core))
+    arrived(held.at[pl.ds(0, 4)], hold_sem.at[0])
+    arrived(held.at[pl.ds(4, 3)], hold_sem.at[1])
+    for n in LATER:
+        core, k, i = place_of(n)
+        send(held.at[n - 5], zr.at[k, c, i], z_sem.at[k], dev(dz=n - 4 if n <= 8 else n - 12, core=core))
 
     def forward(k, h, i):
         if h == 0:
@@ -187,20 +187,22 @@
             for h in range(2):
                 forward(k, h, i)
 
-    def gather_end(k):
+    def project(k, h, line):
+        left = xg[k, h, line].reshape(4 * ROWS, 512)
+        right = wgu[:, pl.ds(pl.multiple_of((line * 2 + h) * 512, 512), 512)]
+        return lax.dot_general(left, right, (((1,), (1,)), ((), ())), preferred_element_type=F32)
+
+    def hidden_of(k):
+        both = project(k, 0, y)
         for j in IN_ORDER[1:]:
-            arrived(xg.at[k, 0, (y - j + 4) % 4], p2_sem.at[k, 0, j - 1])
+            line = (y - j + 4) % 4
+            arrived(xg.at[k, 0, line], p2_sem.at[k, 0, j - 1])
+            both = both + project(k, 0, line)
+        for j in IN_ORDER[1:]:
             arrived(xg.at[k, 1, pl.ds(0, 4), 4 - j], p2_sem.at[k, 1, j - 1])
-
-    def hidden_of(k):
-        gate = up = jnp.zeros((4 * ROWS, 2 * HID), F32)
-        for h in range(2):
-            for line in range(4):
-                left = xg[k, h, line].reshape(4 * ROWS, 512)
-                start = (line * 2 + h) * 512
-                dims = (((1,), (1,)), ((), ()))
-                gate = gate + lax.dot_general(left, wg[:, start:start + 512], dims, preferred_element_type=F32)
-                up = up + lax.dot_general(left, wu[:, start:start + 512], dims, preferred_element_type=F32)
+        for line in range(4):
+            both = both + project(k, 1, line)
+        gate, up = both[:, :2 * HID], both[:, UP:]
         return (gate / (1.0 + jnp.exp(-gate)) * up).astype(BF16)
 
     def spread(k, hidden):
@@ -269,21 +271,23 @@
 
     gather_start(0)
     hand_on(0)
-    gather_start(1)
-    hand_on(1)
     for load in loads[3:]:
         load.wait()
     for copy in to_twin:
         copy.wait_recv()
-    gather_end(0)
+    gather_start(1)
+    hand_on(1)
     spread(0, hidden_of(0))
-    gather_end(1)
     spread(1, hidden_of(1))
     sum_first(0)
     sum_first(1)
     send_back(0)
     send_back(1)
 
+    for copy in sent + to_twin:
+        copy.wait_send()
+    pl.when(c == 1)(to_near.wait_send)
+    pl.when(c == 1)(back_near.wait_send)
     arrived(rb.at[0], back_sem.at[1])
     arrived(rb.at[pl.ds(1, NZ - 1)], back_sem.at[0])
     terms = jnp.dot(mix[...], rb[...].reshape(256, LANES), preferred_element_type=F32)
@@ -291,25 +295,22 @@
     for j in range(PIECES):
         out_ref[:, j * LANES:(j + 1) * LANES] = mixed[j * 16:(j + 1) * 16].astype(BF16)
 
-    for copy in sent + to_twin:
-        copy.wait_send()
-    pl.when(c == 1)(to_near.wait_send)
-    pl.when(c == 1)(back_near.wait_send)
-
 
 def on_device(tokens, expert_ids, route_weights, gate_weight, up_weight, down_weight):
+    operands = (tokens, expert_ids.T, route_weights.T, gate_weight, up_weight, down_weight)
+    operands = [pltpu.with_memory_space_constraint(operand, pltpu.HBM) for operand in operands]
     dma = lambda *shape: pltpu.SemaphoreType.DMA(shape)
     vmem = pltpu.VMEM
     return pl.pallas_call(
         kernel,
-        out_shape=jax.ShapeDtypeStruct((16, 512), BF16),
+        out_shape=pltpu.VMEM((16, 512), BF16),
         in_specs=[pl.BlockSpec(memory_space=pltpu.HBM)] * 6,
         out_specs=pl.BlockSpec(memory_space=pltpu.VMEM),
         scratch_shapes=[
             vmem((16, 512), BF16), vmem((3, 16), jnp.int32), vmem((3, 16), F32),
-            vmem((2 * HID, 4096), BF16), vmem((2 * HID, 4096), BF16), vmem((8, 2 * HID, 512), BF16),
+            vmem((UP + 2 * HID, 4096), BF16), vmem((8, 2 * HID, 512), BF16),
             vmem((16, 16, LANES), BF16), vmem((192, 256), BF16),
-            vmem((4, 16, LANES), BF16), vmem((3, 16, LANES), BF16),
+            vmem((7, 16, LANES), BF16),
             vmem((2, 2, COUNT, 16, LANES), BF16),
             vmem((2, 2, 4, 4, ROWS, 512), BF16),
             vmem((2, 4, ROWS, 512), F32), vmem((2, 4, ROWS, 512), F32),
@@ -318,13 +319,13 @@
             vmem((2, 3, ROWS, 512), BF16), vmem((2, 3, ROWS, 512), BF16),
             vmem((2, 3, ROWS, 512), BF16), vmem((2, 3, ROWS, 512), BF16),
             vmem((2, 2, COUNT, 16, LANES), BF16), vmem((16, 16, LANES), BF16),
-            dma(13), dma(10), dma(10), dma(160), dma(2), dma(2), dma(2), dma(2, 2, 3), dma(2, 2, 3),
+            dma(13), dma(10), dma(10), dma(160), dma(2), dma(2), dma(7), dma(2, 2, 3), dma(2, 2, 3),
             dma(2, 3), dma(2, 3), dma(2, 3), dma(2, 3), dma(2),
         ],
         compiler_params=pltpu.CompilerParams(
-            collective_id=0, has_side_effects=True, vmem_limit_bytes=60 << 20),
+            collective_id=0, has_side_effects=True, vmem_limit_bytes=40 << 20),
         name="experts",
-    )(tokens, expert_ids.T, route_weights.T, gate_weight, up_weight, down_weight)
+    )(*operands)
 
 
 def solution(mesh):

time: 56.3 us -> 54 us (0.959)
  Pallas kernels: 54.8 us -> 53.3 us
  local copies, waits for them, and re-layouts: 1.32 us -> 0.61 us
    pallas_call x1, Pallas kernels: 54.8 us -> 53.3 us  [on_device(): pl.pallas_call(kernel, out_shape=pltpu.VMEM((16, 512), BF16), in_specs=[p...]
    unnamed x1, local copies, waits for them, and re-layouts: 1.32 us -> 0.61 us
where the time goes in v3:
time: 54 us; the launch traced here: 53.9 us
  Pallas kernels  53.3 us (99%)
  local copies, waits for them, and re-layouts  0.61 us (1%)
    pallas_call x1, Pallas kernels, on_device(): pl.pallas_call(kernel, out_shape=pltpu.VMEM((16, 512), BF16), in_specs=[p...  53.3 us

profile of v3, /device:TPU:1, one launch (start us, length us, event | category | flops | bytes accessed | tf_op | source)
XLA Modules:
  0.0 53.9 jit_solution(490127917778089110)
XLA Ops:
  0.0 53.3 %experts.1 = bf16[16,512]{1,0:T(8,128)(2,1)S(1)} custom-call(bf16[16,512]{1,0:T(8,128)(2,1)} %tok_hbm.1, s32[3,16]{1,0:T(4,128)} %bitcast.2, f32[3,16]{1,0:T(4,128)} %bitcast.3, bf16[1,160,4096]{2,1,0:T(8,128)(2,1)} %wg_hbm.1, bf16[1,160,4096]{2,1,0:T(8,128)(2,1)} %wu_hbm.1, bf16[1,160,4096]{2,1,0:T(8,128)(2,1)} %wd_hbm.1), custom_call_target="tpu_custom_call" | custom-call | tf_op jit(solution)/shard_map/experts/pallas_call | solution.py:304
  53.3 0.6 %copy.8 = bf16[16,512]{1,0:T(8,128)(2,1)} copy(bf16[16,512]{1,0:T(8,128)(2,1)S(1)} %experts.1) | data formatting | bytes 32768

commit v4 on v3

--- a/solution.py
+++ b/solution.py
@@ -18,6 +18,7 @@
 ROWS = COUNT * SLOTS
 FAR_FIRST = (2, 1, 3)
 IN_ORDER = (0, 1, 3, 2)
+LAST_OWN = (2, 1, 3, 0)
 LATER = (8, 9, 7, 10, 6, 11, 5)
 
 
@@ -67,7 +68,8 @@
         loads.append(pltpu.make_async_copy(wd_hbm.at[0, :, pl.ds(i * 512, 512)], wd.at[i, pl.ds(0, HID)], load_sem.at[5 + i]))
     for load in loads[:3]:
         load.start()
-    partners = [dict(dz=d, core=core) for d in (4, -4, 3, -3, 2, -2, 1, -1) for core in range(2)]
+    side = 1 - 2 * c
+    partners = [dict(dz=side * d, core=core) for d in (4, 3, 2, 1) for core in range(2)] + [dict(dz=-4 * side)]
     partners += [dict(dx=d) for d in FAR_FIRST] + [dict(dy=d) for d in FAR_FIRST] + [dict(core=1 - c)]
     for partner in partners:
         pl.semaphore_signal(barrier, inc=1, device_id=dev(**partner), device_id_type=MESH)
@@ -206,43 +208,36 @@
         return (gate / (1.0 + jnp.exp(-gate)) * up).astype(BF16)
 
     def spread(k, hidden):
-        for j in FAR_FIRST + (0,):
-            for h in range(2):
-                out = jnp.dot(hidden, wd[(y + j) % 4 * 2 + h], preferred_element_type=F32).reshape(4, ROWS, 512)
-                if h == 0:
-                    own0[k, j] = out[0]
-                    s1x[k, j] = out[1:].astype(BF16)
-                    for i in FAR_FIRST:
-                        send(s1x.at[k, j, i - 1], r1x.at[k, i - 1, j], q1x_sem.at[k, i - 1], dev(dx=i))
-                elif j:
-                    s1y[k, j - 1] = out.astype(BF16)
-                    send(s1y.at[k, j - 1], r1y.at[k, j - 1], q1y_sem.at[k, j - 1], dev(dy=j))
+        for j in LAST_OWN:
+            out = jnp.dot(hidden, wd[(y + j) % 4 * 2], preferred_element_type=F32).reshape(4, ROWS, 512)
+            own0[k, j] = out[0]
+            s1x[k, j] = out[1:].astype(BF16)
+            for i in FAR_FIRST:
+                send(s1x.at[k, j, i - 1], r1x.at[k, i - 1, j], q1x_sem.at[k, i - 1, j], dev(dx=i))
+            out = jnp.dot(hidden, wd[(y + j) % 4 * 2 + 1], preferred_element_type=F32).reshape(4, ROWS, 512)
+            if j:
+                s1y[k, j - 1] = out.astype(BF16)
+            else:
+                own1[k] = out
+            if j == 3:
+                for i in LAST_OWN:
+                    for n in FAR_FIRST:
+                        send(s1y.at[k, n - 1, i], r1y.at[k, n - 1, i], q1y_sem.at[k, n - 1, i], dev(dy=n))
+
+    def sum_first(k):
+        for i in LAST_OWN:
+            for own, landed, sem, out, last, last_sem in (
+                    (own1, r1y, q1y_sem, s2y, r2y, q2y_sem), (own0, r1x, q1x_sem, s2x, r2x, q2x_sem)):
+                total = own[k, i]
+                for n in FAR_FIRST:
+                    arrived(landed.at[k, n - 1, i], sem.at[k, n - 1, i])
+                    total = total + landed[k, n - 1, i].astype(F32)
+                if i:
+                    out[k, i - 1] = total.astype(BF16)
+                    device = dev(dx=i) if own is own1 else dev(dy=i)
+                    send(out.at[k, i - 1], last.at[k, i - 1], last_sem.at[k, i - 1], device)
                 else:
-                    own1[k] = out
-
-    def sum_first(k):
-        for n in range(3):
-            arrived(r1y.at[k, n], q1y_sem.at[k, n])
-        for i in FAR_FIRST + (0,):
-            total = own1[k, i]
-            for n in range(3):
-                total = total + r1y[k, n, i].astype(F32)
-            if i:
-                s2y[k, i - 1] = total.astype(BF16)
-                send(s2y.at[k, i - 1], r2y.at[k, i - 1], q2y_sem.at[k, i - 1], dev(dx=i))
-            else:
-                own1[k, 0] = total
-        for n in range(3):
-            arrived(r1x.at[k, n], q1x_sem.at[k, n])
-        for j in FAR_FIRST + (0,):
-            total = own0[k, j]
-            for n in range(3):
-                total = total + r1x[k, n, j].astype(F32)
-            if j:
-                s2x[k, j - 1] = total.astype(BF16)
-                send(s2x.at[k, j - 1], r2x.at[k, j - 1], q2x_sem.at[k, j - 1], dev(dy=j))
-            else:
-                own0[k, 0] = total
+                    own[k, 0] = total
 
     def send_back(k):
         for h, own, landed, sem in ((1, own1, r2y, q2y_sem), (0, own0, r2x, q2x_sem)):
@@ -320,7 +315,7 @@
             vmem((2, 3, ROWS, 512), BF16), vmem((2, 3, ROWS, 512), BF16),
             vmem((2, 2, COUNT, 16, LANES), BF16), vmem((16, 16, LANES), BF16),
             dma(13), dma(10), dma(10), dma(160), dma(2), dma(2), dma(7), dma(2, 2, 3), dma(2, 2, 3),
-            dma(2, 3), dma(2, 3), dma(2, 3), dma(2, 3), dma(2),
+            dma(2, 3, 4), dma(2, 3, 4), dma(2, 3), dma(2, 3), dma(2),
         ],
         compiler_params=pltpu.CompilerParams(
             collective_id=0, has_side_effects=True, vmem_limit_bytes=40 << 20),

time: 54 us -> 53.6 us (level)
  no operation moved by 1% of the time
where the time goes in v4:
time: 53.6 us; the launch traced here: 53.5 us
  Pallas kernels  52.9 us (99%)
  local copies, waits for them, and re-layouts  0.61 us (1%)
    pallas_call x1, Pallas kernels, on_device(): pl.pallas_call(kernel, out_shape=pltpu.VMEM((16, 512), BF16), in_specs=[p...  52.9 us

profile of v4, /device:TPU:1, one launch (start us, length us, event | category | flops | bytes accessed | tf_op | source)
XLA Modules:
  0.0 53.5 jit_solution(8605110877459535318)
XLA Ops:
  0.0 52.9 %experts.1 = bf16[16,512]{1,0:T(8,128)(2,1)S(1)} custom-call(bf16[16,512]{1,0:T(8,128)(2,1)} %tok_hbm.1, s32[3,16]{1,0:T(4,128)} %bitcast.2, f32[3,16]{1,0:T(4,128)} %bitcast.3, bf16[1,160,4096]{2,1,0:T(8,128)(2,1)} %wg_hbm.1, bf16[1,160,4096]{2,1,0:T(8,128)(2,1)} %wu_hbm.1, bf16[1,160,4096]{2,1,0:T(8,128)(2,1)} %wd_hbm.1), custom_call_target="tpu_custom_call" | custom-call | tf_op jit(solution)/shard_map/experts/pallas_call | solution.py:299
  52.9 0.6 %copy.8 = bf16[16,512]{1,0:T(8,128)(2,1)} copy(bf16[16,512]{1,0:T(8,128)(2,1)S(1)} %experts.1) | data formatting | bytes 32768
